TPU v7x, 256 devices: a whole 4x4x8 slice. The times are simulated.
256 devices in a mesh: band: 32 (over x, y, core), field: 8 (over z).
Axes of the slice: x: 4, y: 4, z: 8, core: 2. Of those that a mesh axis runs over, the one named last changes fastest.
Arguments:
- column_state: bfloat16 [512, 1280, 256], P(('band', 'field')), may hold values from -6 to 6
- cosine: float32 [512, 1280], P(('band', 'field')), may hold values from 0.2 to 1
- sunlit: int32 [512, 1280], P(('band', 'field')), may hold values from 0 to 1, as said below
- w_in: bfloat16 [256, 2048], replicated, may hold values from -0.375 to 0.375
- w_out: bfloat16 [2048, 128], replicated, may hold values from -0.125 to 0.125
- w_long: bfloat16 [256, 128], replicated, may hold values from -0.375 to 0.375
- fourier: bfloat16 [512, 32, 2, 4, 128], P('band', None, None, None, 'field'), may hold values from -6 to 6
- quadrature: float32 [512], P('band'), may hold values from 0.5 to 2
- legendre: bfloat16 [32, 640, 512], P('band'), may hold values from -0.25 to 0.25
- damping: float32 [32, 640], P('band'), may hold values from 0.1 to 1
Outputs:
- heating: bfloat16 [512, 1280, 128], P(('band', 'field'))
- updated: bfloat16 [512, 32, 2, 4, 128], P('band', None, None, None, 'field')
Inputs may be any that keep to these rules, and one draw needn't show every extreme that they name: Sunlit columns form whole blocks of 32 columns along a latitude. Latitude rows come north then south, each ordered from the pole; row r and row r + 256 have 40 sunlit blocks together.
All inputs are finite; a program needn't handle non-finite values.
Results may differ from a plain program's by a relative error of at most 0.0055.
Values may be sent and summed in bfloat16 or wider, within the bound.
A program may use at most 64 MiB of HBM per device.

v0:
```python
import jax
import jax.numpy as jnp
from jax import lax
from jax.sharding import PartitionSpec as P

BCOL = 32


def short_wave(blocks_state, w_in, w_out):
    hidden = jax.nn.gelu(
        jnp.einsum("bcf,fh->bch", blocks_state, w_in, preferred_element_type=jnp.float32)
    ).astype(jnp.bfloat16)
    return jnp.einsum("bch,hl->bcl", hidden, w_out, preferred_element_type=jnp.float32).astype(
        jnp.bfloat16
    )


def fourier_table(count_lon, count_wave):
    longitude = jnp.arange(count_lon, dtype=jnp.int32)
    wavenumber = jnp.arange(count_wave, dtype=jnp.int32)
    phase = longitude[:, None] * wavenumber[None, :] % count_lon
    angle = 2.0 * jnp.pi / count_lon * phase.astype(jnp.float32)
    scale = 1.0 / jnp.sqrt(jnp.float32(count_lon))
    return jnp.concatenate([jnp.cos(angle), -jnp.sin(angle)], axis=1) * scale


def local(
    column_state, cosine, sunlit, w_in, w_out, w_long, fourier, quadrature, legendre, damping
):
    row_count, lon_count, feat_count = column_state.shape
    level_count = w_out.shape[1]
    block_count = row_count * lon_count // BCOL
    flat_state = column_state.reshape(row_count * lon_count, feat_count)
    long_wave = jnp.dot(flat_state, w_long, preferred_element_type=jnp.float32)
    blocks_state = column_state.reshape(block_count, BCOL, feat_count)
    short_blocks = short_wave(blocks_state, w_in, w_out)
    short_flat = short_blocks.reshape(row_count * lon_count, level_count)
    lighting = (sunlit.astype(jnp.float32) * cosine).reshape(row_count * lon_count)
    heating = (long_wave + lighting[:, None] * short_flat.astype(jnp.float32)).astype(jnp.bfloat16)
    heating = heating.reshape(row_count, lon_count, level_count)
    gathered = lax.all_to_all(heating, "field", split_axis=2, concat_axis=0, tiled=True)
    lat_count, wave_count = (fourier.shape[0], fourier.shape[1])
    level_local = fourier.shape[4]
    table = fourier_table(lon_count, wave_count)
    heat_fourier = jnp.einsum(
        "alv,lk->akv", gathered.astype(jnp.float32), table, precision=lax.Precision.HIGHEST
    )
    heat_fourier = heat_fourier.reshape(lat_count, 2, wave_count, level_local).transpose(0, 2, 1, 3)
    warm = fourier.astype(jnp.float32).at[:, :, :, 2, :].add(heat_fourier)
    sent = (quadrature[:, None, None, None, None] * warm).astype(jnp.bfloat16)
    outputs = []
    for field_index in range(4):
        single = sent[:, :, :, field_index, :].reshape(lat_count, wave_count, 2 * level_local)
        spectral = jnp.einsum(
            "mnl,lmc->mnc",
            legendre,
            lax.all_to_all(single, "band", split_axis=1, concat_axis=0, tiled=True),
            preferred_element_type=jnp.float32,
        )
        damped = (spectral * damping[:, :, None]).astype(jnp.bfloat16)
        moved = lax.all_to_all(
            jnp.einsum("mnl,mnc->lmc", legendre, damped, preferred_element_type=jnp.float32).astype(
                jnp.bfloat16
            ),
            "band",
            split_axis=0,
            concat_axis=1,
            tiled=True,
        )
        outputs.append(moved.reshape(lat_count, wave_count, 2, level_local))
    updated = jnp.stack(outputs, axis=3)
    return (heating, updated)


def solution(mesh):
    in_specs = (
        P(("band", "field"), None, None),
        P(("band", "field"), None),
        P(("band", "field"), None),
        P(),
        P(),
        P(),
        P("band", None, None, None, "field"),
        P("band"),
        P("band", None, None),
        P("band", None),
    )
    out_specs = (P(("band", "field"), None, None), P("band", None, None, None, "field"))
    return jax.shard_map(local, mesh=mesh, in_specs=in_specs, out_specs=out_specs, check_vma=False)
```

profile of v0, /device:TPU:1, one launch (start us, length us, event | category | flops | bytes accessed | tf_op | source)
XLA Modules:
  0.0 140.3 jit_solution(15925864603128986389)
XLA Ops:
  0.6 0.8 convert_multiply_fusion.1
  1.5 0.5 copy-done
  2.0 8.5 %fusion.13 = bf16[80,32,128]{2,1,0:T(8,128)(2,1)S(1)} fusion(bf16[80,32,256]{2,1,0:T(8,128)(2,1)S(1)} %bitcast.115, bf16[256,2048]{1,0:T(8,128)(2,1)} %param.15, bf16[2048,128]{1,0:T(8,128)(2,1)} %param.16), kind=kOutput, calls=%fused_computation.13 | convolution fusion | flops 4074045440 | bytes 3538944 | tf_op jit(solution)/shard_map/bch,hl->bcl/dot_general | solution.py:13
  10.5 0.5 fusion.12
  11.0 1.9 %copy.49 = bf16[2,1280,128]{1,0,2:T(2,128)(2,1)} copy(bf16[2,1280,128]{2,1,0:T(8,128)(2,1)S(1)} %bitcast.118) | data formatting | bytes 1310720 | tf_op jit(solution)/shard_map/reshape | solution.py:40
  12.9 9.0 %all-to-all-start = ((bf16[2,1280,128]{1,0,2:T(2,128)(2,1)}), bf16[2,1280,128]{1,0,2:T(2,128)(2,1)S(1)}, u32[]{:S(2)}, u32[]{:S(2)}) async-start(bf16[2,1280,128]{1,0,2:T(2,128)(2,1)} %copy.49), calls=%async_computation | async-start | bytes 1310720 | tf_op jit(solution)/shard_map/all_to_all | solution.py:41
  22.1 0.7 sine_negate_fusion
  22.8 20.0 %all-to-all-done = bf16[2,1280,128]{1,0,2:T(2,128)(2,1)S(1)} async-done(((bf16[2,1280,128]{1,0,2:T(2,128)(2,1)}), bf16[2,1280,128]{1,0,2:T(2,128)(2,1)S(1)}, u32[]{:S(2)}, u32[]{:S(2)}) %all-to-all-start) | async-done | bytes 655392 | tf_op jit(solution)/shard_map/all_to_all | solution.py:41
  42.9 0.7 fusion.35
  43.6 0.2 reshape.127
  43.8 0.2 multiply_convert_fusion
  44.1 0.2 copy.53
  44.2 0.8 reshape.152
  45.0 7.6 %all-to-all-start.1 = ((bf16[32,2,256]{2,1,0:T(2,128)(2,1)}), bf16[32,2,256]{2,1,0:T(2,128)(2,1)S(1)}, u32[]{:S(2)}, u32[]{:S(2)}) async-start(bf16[32,2,256]{2,1,0:T(2,128)(2,1)} %reshape.152), calls=%async_computation.1 | async-start | bytes 65536 | tf_op jit(solution)/shard_map/all_to_all | solution.py:57
  52.6 0.2 copy.56
  52.8 0.8 reshape.148
  53.5 6.3 %all-to-all-done.1 = bf16[32,2,256]{2,1,0:T(2,128)(2,1)S(1)} async-done(((bf16[32,2,256]{2,1,0:T(2,128)(2,1)}), bf16[32,2,256]{2,1,0:T(2,128)(2,1)S(1)}, u32[]{:S(2)}, u32[]{:S(2)}) %all-to-all-start.1) | async-done | bytes 32800 | tf_op jit(solution)/shard_map/all_to_all | solution.py:57
  59.9 3.9 %all-to-all-start.3 = ((bf16[32,2,256]{2,1,0:T(2,128)(2,1)}), bf16[32,2,256]{2,1,0:T(2,128)(2,1)S(1)}, u32[]{:S(2)}, u32[]{:S(2)}) async-start(bf16[32,2,256]{2,1,0:T(2,128)(2,1)} %reshape.148), calls=%async_computation.3 | async-start | bytes 65536 | tf_op jit(solution)/shard_map/all_to_all | solution.py:57
  63.8 0.2 copy.59
  63.9 0.8 reshape.144
  64.7 6.5 %all-to-all-done.3 = bf16[32,2,256]{2,1,0:T(2,128)(2,1)S(1)} async-done(((bf16[32,2,256]{2,1,0:T(2,128)(2,1)}), bf16[32,2,256]{2,1,0:T(2,128)(2,1)S(1)}, u32[]{:S(2)}, u32[]{:S(2)}) %all-to-all-start.3) | async-done | bytes 32800 | tf_op jit(solution)/shard_map/all_to_all | solution.py:57
  71.2 4.0 %all-to-all-start.5 = ((bf16[32,2,256]{2,1,0:T(2,128)(2,1)}), bf16[32,2,256]{2,1,0:T(2,128)(2,1)S(1)}, u32[]{:S(2)}, u32[]{:S(2)}) async-start(bf16[32,2,256]{2,1,0:T(2,128)(2,1)} %reshape.144), calls=%async_computation.5 | async-start | bytes 65536 | tf_op jit(solution)/shard_map/all_to_all | solution.py:57
  75.2 0.2 copy.62
  75.4 0.8 reshape.140
  76.1 0.1 reshape.153
  76.3 6.3 %all-to-all-done.5 = bf16[32,2,256]{2,1,0:T(2,128)(2,1)S(1)} async-done(((bf16[32,2,256]{2,1,0:T(2,128)(2,1)}), bf16[32,2,256]{2,1,0:T(2,128)(2,1)S(1)}, u32[]{:S(2)}, u32[]{:S(2)}) %all-to-all-start.5) | async-done | bytes 32800 | tf_op jit(solution)/shard_map/all_to_all | solution.py:57
  82.6 3.9 %all-to-all-start.7 = ((bf16[32,2,256]{2,1,0:T(2,128)(2,1)}), bf16[32,2,256]{2,1,0:T(2,128)(2,1)S(1)}, u32[]{:S(2)}, u32[]{:S(2)}) async-start(bf16[32,2,256]{2,1,0:T(2,128)(2,1)} %reshape.140), calls=%async_computation.7 | async-start | bytes 65536 | tf_op jit(solution)/shard_map/all_to_all | solution.py:57
  86.5 0.4 fusion.20
  86.9 0.6 broadcast.32
  87.5 0.6 reduce.6
  88.1 0.1 copy.74
  88.3 0.8 reshape.154
  89.0 0.1 reshape.149
  89.1 4.7 %all-to-all-done.7 = bf16[32,2,256]{2,1,0:T(2,128)(2,1)S(1)} async-done(((bf16[32,2,256]{2,1,0:T(2,128)(2,1)}), bf16[32,2,256]{2,1,0:T(2,128)(2,1)S(1)}, u32[]{:S(2)}, u32[]{:S(2)}) %all-to-all-start.7) | async-done | bytes 32800 | tf_op jit(solution)/shard_map/all_to_all | solution.py:57
  93.9 3.8 %all-to-all-start.2 = ((bf16[32,2,256]{2,1,0:T(2,128)(2,1)}), bf16[32,2,256]{2,1,0:T(2,128)(2,1)S(1)}, u32[]{:S(2)}, u32[]{:S(2)}) async-start(bf16[32,2,256]{2,1,0:T(2,128)(2,1)} %reshape.154), calls=%async_computation.2 | async-start | bytes 65536 | tf_op jit(solution)/shard_map/all_to_all | solution.py:61
  97.7 0.4 fusion.21
  98.1 0.7 reduce.5
  98.8 0.1 copy.73
  98.9 0.8 reshape.150
  99.7 0.1 reshape.145
  99.8 5.3 %all-to-all-done.2 = bf16[32,2,256]{2,1,0:T(2,128)(2,1)S(1)} async-done(((bf16[32,2,256]{2,1,0:T(2,128)(2,1)}), bf16[32,2,256]{2,1,0:T(2,128)(2,1)S(1)}, u32[]{:S(2)}, u32[]{:S(2)}) %all-to-all-start.2) | async-done | bytes 32800 | tf_op jit(solution)/shard_map/all_to_all | solution.py:61
  105.1 3.9 %all-to-all-start.4 = ((bf16[32,2,256]{2,1,0:T(2,128)(2,1)}), bf16[32,2,256]{2,1,0:T(2,128)(2,1)S(1)}, u32[]{:S(2)}, u32[]{:S(2)}) async-start(bf16[32,2,256]{2,1,0:T(2,128)(2,1)} %reshape.150), calls=%async_computation.4 | async-start | bytes 65536 | tf_op jit(solution)/shard_map/all_to_all | solution.py:61
  109.0 0.4 fusion.22
  109.4 0.7 reduce.4
  110.2 0.8 reshape.146
  111.0 0.1 reshape.141
  111.1 5.3 %all-to-all-done.4 = bf16[32,2,256]{2,1,0:T(2,128)(2,1)S(1)} async-done(((bf16[32,2,256]{2,1,0:T(2,128)(2,1)}), bf16[32,2,256]{2,1,0:T(2,128)(2,1)S(1)}, u32[]{:S(2)}, u32[]{:S(2)}) %all-to-all-start.4) | async-done | bytes 32800 | tf_op jit(solution)/shard_map/all_to_all | solution.py:61
  116.4 3.8 %all-to-all-start.6 = ((bf16[32,2,256]{2,1,0:T(2,128)(2,1)}), bf16[32,2,256]{2,1,0:T(2,128)(2,1)S(1)}, u32[]{:S(2)}, u32[]{:S(2)}) async-start(bf16[32,2,256]{2,1,0:T(2,128)(2,1)} %reshape.146), calls=%async_computation.6 | async-start | bytes 65536 | tf_op jit(solution)/shard_map/all_to_all | solution.py:61
  120.2 0.4 fusion.23
  120.7 0.7 reduce.3
  121.4 0.8 reshape.142
  122.2 5.4 %all-to-all-done.6 = bf16[32,2,256]{2,1,0:T(2,128)(2,1)S(1)} async-done(((bf16[32,2,256]{2,1,0:T(2,128)(2,1)}), bf16[32,2,256]{2,1,0:T(2,128)(2,1)S(1)}, u32[]{:S(2)}, u32[]{:S(2)}) %all-to-all-start.6) | async-done | bytes 32800 | tf_op jit(solution)/shard_map/all_to_all | solution.py:61
  127.6 3.9 %all-to-all-start.8 = ((bf16[32,2,256]{2,1,0:T(2,128)(2,1)}), bf16[32,2,256]{2,1,0:T(2,128)(2,1)S(1)}, u32[]{:S(2)}, u32[]{:S(2)}) async-start(bf16[32,2,256]{2,1,0:T(2,128)(2,1)} %reshape.142), calls=%async_computation.8 | async-start | bytes 65536 | tf_op jit(solution)/shard_map/all_to_all | solution.py:61
  131.5 0.2 reshape.155
  131.7 0.2 copy.55
  131.9 0.2 reshape.151
  132.1 0.2 copy.58
  132.3 0.2 reshape.147
  132.5 0.2 copy.61
  132.6 6.3 %all-to-all-done.8 = bf16[32,2,256]{2,1,0:T(2,128)(2,1)S(1)} async-done(((bf16[32,2,256]{2,1,0:T(2,128)(2,1)}), bf16[32,2,256]{2,1,0:T(2,128)(2,1)S(1)}, u32[]{:S(2)}, u32[]{:S(2)}) %all-to-all-start.8) | async-done | bytes 32800 | tf_op jit(solution)/shard_map/all_to_all | solution.py:61
  138.9 0.2 reshape.143
  139.1 0.2 copy.64
  139.3 0.1 pad_maximum_fusion
  139.4 0.9 copy.65
  (26 shorter events, 0.7 us)
Async XLA Ops:
  0.6 1.4 copy-start
  2.0 8.5 %copy-start.4 = (bf16[256,128]{1,0:T(8,128)(2,1)S(1)}, bf16[256,128]{1,0:T(8,128)(2,1)}, u32[]{:S(2)}) copy-start(bf16[256,128]{1,0:T(8,128)(2,1)} %param.17) | copy-start | bytes 196612
  11.0 1.9 %copy-start.2 = (bf16[2560,128]{1,0:T(8,128)(2,1)}, bf16[2560,128]{1,0:T(8,128)(2,1)S(1)}, u32[]{:S(2)}) copy-start(bf16[2560,128]{1,0:T(8,128)(2,1)S(1)} %fusion.12) | copy-start | bytes 1966084
  11.0 10.9 %copy-start.3 = (bf16[16,32,2,4,16]{1,4,3,2,0:T(8,128)(2,1)S(1)}, bf16[16,32,2,4,16]{1,4,3,2,0:T(8,128)(2,1)}, u32[]{:S(2)}) copy-start(bf16[16,32,2,4,16]{1,4,3,2,0:T(8,128)(2,1)} %param.18) | copy-start | bytes 393220
  12.9 29.8 %all-to-all-start = ((bf16[2,1280,128]{1,0,2:T(2,128)(2,1)}), bf16[2,1280,128]{1,0,2:T(2,128)(2,1)S(1)}, u32[]{:S(2)}, u32[]{:S(2)}) async-start(bf16[2,1280,128]{1,0,2:T(2,128)(2,1)} %copy.49), calls=%async_computation | async-start | bytes 1310720 | tf_op jit(solution)/shard_map/all_to_all | solution.py:41
  42.9 1.0 copy-start.6
  44.0 31.2 %copy-start.5 = (f32[1,640]{1,0:T(1,128)S(1)}, f32[1,640]{1,0:T(1,128)}, u32[]{:S(2)}) copy-start(f32[1,640]{1,0:T(1,128)} %param.21) | copy-start | bytes 7684
  44.1 42.4 %copy-start.1 = (bf16[1,640,512]{2,1,0:T(8,128)(2,1)S(1)}, bf16[1,640,512]{2,1,0:T(8,128)(2,1)}, u32[]{:S(2)}) copy-start(bf16[1,640,512]{2,1,0:T(8,128)(2,1)} %param.20) | copy-start | bytes 1966084
  45.0 14.9 %all-to-all-start.1 = ((bf16[32,2,256]{2,1,0:T(2,128)(2,1)}), bf16[32,2,256]{2,1,0:T(2,128)(2,1)S(1)}, u32[]{:S(2)}, u32[]{:S(2)}) async-start(bf16[32,2,256]{2,1,0:T(2,128)(2,1)} %reshape.152), calls=%async_computation.1 | async-start | bytes 65536 | tf_op jit(solution)/shard_map/all_to_all | solution.py:57
  59.9 11.3 %all-to-all-start.3 = ((bf16[32,2,256]{2,1,0:T(2,128)(2,1)}), bf16[32,2,256]{2,1,0:T(2,128)(2,1)S(1)}, u32[]{:S(2)}, u32[]{:S(2)}) async-start(bf16[32,2,256]{2,1,0:T(2,128)(2,1)} %reshape.148), calls=%async_computation.3 | async-start | bytes 65536 | tf_op jit(solution)/shard_map/all_to_all | solution.py:57
  71.2 11.4 %all-to-all-start.5 = ((bf16[32,2,256]{2,1,0:T(2,128)(2,1)}), bf16[32,2,256]{2,1,0:T(2,128)(2,1)S(1)}, u32[]{:S(2)}, u32[]{:S(2)}) async-start(bf16[32,2,256]{2,1,0:T(2,128)(2,1)} %reshape.144), calls=%async_computation.5 | async-start | bytes 65536 | tf_op jit(solution)/shard_map/all_to_all | solution.py:57
  82.6 11.3 %all-to-all-start.7 = ((bf16[32,2,256]{2,1,0:T(2,128)(2,1)}), bf16[32,2,256]{2,1,0:T(2,128)(2,1)S(1)}, u32[]{:S(2)}, u32[]{:S(2)}) async-start(bf16[32,2,256]{2,1,0:T(2,128)(2,1)} %reshape.140), calls=%async_computation.7 | async-start | bytes 65536 | tf_op jit(solution)/shard_map/all_to_all | solution.py:57
  93.9 11.2 %all-to-all-start.2 = ((bf16[32,2,256]{2,1,0:T(2,128)(2,1)}), bf16[32,2,256]{2,1,0:T(2,128)(2,1)S(1)}, u32[]{:S(2)}, u32[]{:S(2)}) async-start(bf16[32,2,256]{2,1,0:T(2,128)(2,1)} %reshape.154), calls=%async_computation.2 | async-start | bytes 65536 | tf_op jit(solution)/shard_map/all_to_all | solution.py:61
  105.1 11.3 %all-to-all-start.4 = ((bf16[32,2,256]{2,1,0:T(2,128)(2,1)}), bf16[32,2,256]{2,1,0:T(2,128)(2,1)S(1)}, u32[]{:S(2)}, u32[]{:S(2)}) async-start(bf16[32,2,256]{2,1,0:T(2,128)(2,1)} %reshape.150), calls=%async_computation.4 | async-start | bytes 65536 | tf_op jit(solution)/shard_map/all_to_all | solution.py:61
  116.4 11.2 %all-to-all-start.6 = ((bf16[32,2,256]{2,1,0:T(2,128)(2,1)}), bf16[32,2,256]{2,1,0:T(2,128)(2,1)S(1)}, u32[]{:S(2)}, u32[]{:S(2)}) async-start(bf16[32,2,256]{2,1,0:T(2,128)(2,1)} %reshape.146), calls=%async_computation.6 | async-start | bytes 65536 | tf_op jit(solution)/shard_map/all_to_all | solution.py:61
  127.6 11.3 %all-to-all-start.8 = ((bf16[32,2,256]{2,1,0:T(2,128)(2,1)}), bf16[32,2,256]{2,1,0:T(2,128)(2,1)S(1)}, u32[]{:S(2)}, u32[]{:S(2)}) async-start(bf16[32,2,256]{2,1,0:T(2,128)(2,1)} %reshape.142), calls=%async_computation.8 | async-start | bytes 65536 | tf_op jit(solution)/shard_map/all_to_all | solution.py:61
where the time goes:
time: 141 us; the launch traced here: 140 us
  waiting for transfers between devices  65.9 us (47%)
  starting transfers between devices  43.9 us (31%)
  local copies, waits for them, and re-layouts  13.4 us (10%)
  matrix products  11.4 us (8%)
  other arithmetic  4.61 us (3%)
    all_to_all x4, waiting for transfers between devices, local(): lax.all_to_all(single, 'band', split_axis=1, concat_axis=0, tiled=True)  23.8 us
    all_to_all x4, waiting for transfers between devices, local(): lax.all_to_all(jnp.einsum('mnl,mnc->lmc', legendre, damped, preferred_ele...  22.2 us
    all_to_all x1, waiting for transfers between devices, local(): lax.all_to_all(heating, 'field', split_axis=2, concat_axis=0, tiled=True)  20 us
    all_to_all x4, starting transfers between devices, local(): lax.all_to_all(single, 'band', split_axis=1, concat_axis=0, tiled=True)  19.4 us
    all_to_all x4, starting transfers between devices, local(): lax.all_to_all(jnp.einsum('mnl,mnc->lmc', legendre, damped, preferred_ele...  15.5 us
    unnamed x39, local copies, waits for them, and re-layouts  9.17 us
    all_to_all x1, starting transfers between devices, local(): lax.all_to_all(heating, 'field', split_axis=2, concat_axis=0, tiled=True)  9.02 us
    dot_general x1, matrix products, short_wave(): jnp.einsum('bch,hl->bcl', hidden, w_out, preferred_element_type=jnp.float32)  8.48 us
  transfers between devices with their start and end apart: 9, of which 9 were waited for; matrix products, arithmetic and copies ran while one was open for 10% of the time, Pallas kernels for 0%

commit v1 on v0

v1 whole, which is shorter than its diff:
```python
import functools

import jax
import jax.numpy as jnp
import ml_dtypes
import numpy as np
from jax import lax
from jax.experimental import pallas as pl
from jax.experimental.pallas import tpu as pltpu
from jax.sharding import PartitionSpec as P

F32 = jnp.float32
BF16 = jnp.bfloat16
LON = 1280
WAVES = 32
CHUNK = 256
HCHUNK = 512
MESH = pl.DeviceIdType.MESH
GELU_A = 0.7978845608028654
GELU_B = 0.7978845608028654 * 0.044715


def nt(a, b):
    return lax.dot_general(a, b, (((1,), (1,)), ((), ())), preferred_element_type=F32)


def nn(a, b):
    return jnp.dot(a, b, preferred_element_type=F32)


def fourier_rows():
    phase = np.arange(LON)[None, :] * np.arange(WAVES)[:, None] % LON
    angle = 2.0 * np.pi / LON * phase
    full = np.stack([np.cos(angle), -np.sin(angle)], axis=1) / np.sqrt(LON)
    high = full.astype(ml_dtypes.bfloat16)
    low = (full - high.astype(np.float64)).astype(ml_dtypes.bfloat16)
    return np.stack([high, low], axis=1).reshape(4 * WAVES, LON)


def gelu2(x):
    x = x.astype(BF16)
    inner = x * (x * x * BF16(GELU_B) + BF16(GELU_A))
    return x + x * jnp.tanh(inner)


def radiation(
    state, cosine, sunlit, w_in, w_out, w_long, table, heating, packed, half_out, light, acc
):
    half_out[...] = (w_out[...].astype(F32) * 0.5).astype(BF16)
    lit = sunlit[...].astype(F32) * cosine[...]
    rows = jnp.concatenate(
        [lit[:, j * 128 : (j + 1) * 128] for j in range(10)] + [jnp.zeros((108, 128), F32)], axis=0
    )
    light[...] = rows.T
    acc[...] = jnp.zeros_like(acc)
    lane = lax.broadcasted_iota(jnp.int32, (128, 128), 1)

    def step(index, carry):
        row = index // 5
        part = index % 5
        here = pl.ds(pl.multiple_of(index * CHUNK, CHUNK), CHUNK)
        x = state[here, :]
        short = jnp.zeros((CHUNK, 128), F32)
        for h in range(0, 2048, HCHUNK):
            hidden = gelu2(nn(x, w_in[:, h : h + HCHUNK]))
            short = short + nn(hidden, half_out[h : h + HCHUNK, :])
        long = nn(x, w_long[...])
        scale = []
        for g in range(2):
            wanted = (part * 2 + g) * 2 + row
            scale.append(jnp.sum(jnp.where(lane == wanted, light[...], 0.0), axis=1, keepdims=True))
        scale = jnp.concatenate(scale, axis=0)
        heat = (long + scale * short.astype(BF16).astype(F32)).astype(BF16)
        heating[here, :] = heat
        cols = pl.ds(pl.multiple_of(part * CHUNK, CHUNK), CHUNK)
        acc[row] += nn(table[:, cols], heat)
        return carry

    lax.fori_loop(0, 10, step, 0)
    first, second = acc[0], acc[1]
    wave_row = lax.broadcasted_iota(jnp.int32, (128, 128), 0)
    both = jnp.where(
        (wave_row % 4) < 2,
        first + pltpu.roll(first, 126, 0),
        second + pltpu.roll(second, 2, 0),
    )
    packed[...] = both.T.astype(BF16).reshape(8, 16, 128)


def spectral_kernel(
    packed, fourier, quad, legendre, damping, updated,
    field_in, send1, recv1, back1, home1, send2, recv2, back2, home2,
    trans, tall, wide, leg_p, leg_t, damp, send_sems, recv_sems,
):
    band = lax.axis_index("band")
    field = lax.axis_index("field")

    barrier = pltpu.get_barrier_semaphore()

    def greet_band(step, carry):
        other = lax.rem(band + step, 32)
        pl.semaphore_signal(barrier, inc=1, device_id=(other, field), device_id_type=MESH)
        return carry

    def greet_field(step, carry):
        other = lax.rem(field + step, 8)
        pl.semaphore_signal(barrier, inc=1, device_id=(band, other), device_id_type=MESH)
        return carry

    lax.fori_loop(1, 8, greet_field, 0)
    lax.fori_loop(1, 32, greet_band, 0)

    def exchange_field(source, target, slot):
        def one(step, carry):
            other = lax.rem(field + step, 8)
            pltpu.make_async_remote_copy(
                src_ref=source.at[other], dst_ref=target.at[field],
                send_sem=send_sems.at[slot], recv_sem=recv_sems.at[slot],
                device_id=(band, other), device_id_type=MESH,
            ).start()
            return carry

        lax.fori_loop(1, 8, one, 0)
        target[field] = source[field]

    def exchange_band(source, target, slot):
        def one(step, carry):
            other = lax.rem(band + step, 32)
            pltpu.make_async_remote_copy(
                src_ref=source.at[other], dst_ref=target.at[band],
                send_sem=send_sems.at[slot], recv_sem=recv_sems.at[slot],
                device_id=(other, field), device_id_type=MESH,
            ).start()
            return carry

        lax.fori_loop(1, 32, one, 0)
        target[band] = source[band]

    def arrived(target, slot, count):
        part = target.at[pl.ds(0, count)]
        pltpu.make_async_copy(part, part, recv_sems.at[slot]).wait()

    def gone(source, slot, count):
        part = source.at[pl.ds(0, count)]
        pltpu.make_async_copy(part, part, send_sems.at[slot]).wait()

    pl.semaphore_wait(barrier, 38)
    exchange_field(packed, field_in, 0)

    eye = (
        lax.broadcasted_iota(jnp.int32, (32, 32), 0) == lax.broadcasted_iota(jnp.int32, (32, 32), 1)
    ).astype(BF16)
    waves = nt(eye, fourier[...])
    lane = lax.broadcasted_iota(jnp.int32, (32, 128), 1)
    for l in range(16):
        trans[pl.ds(l, 32, stride=16), :] = waves[:, l * 128 : (l + 1) * 128] * quad[l]
    send1[...] = trans[...].astype(BF16).reshape(32, 16, 128)
    exchange_band(send1, recv1, 1)

    for row in range(2):
        weight = jnp.zeros((32, 128), F32)
        for z in range(8):
            weight = jnp.where(lane // 16 == z, quad[z * 2 + row], weight)
        for part in range(2):
            k = row * 2 + part
            piece = jnp.zeros((32, 128), F32)
            for z in range(8):
                at = (z * 2 + row) * 128 + part * 64 + 32
                block = waves[:, at // 128 * 128 : at // 128 * 128 + 128]
                moved = pltpu.roll(block, (16 * z - at % 128) % 128, 1)
                piece = jnp.where(lane // 16 == z, moved, piece)
            wide[0, pl.ds(k, 32, stride=4), :] = piece
            wide[1, pl.ds(k, 32, stride=4), :] = weight

    lat = lax.broadcasted_iota(jnp.int32, (512, 512), 0)
    order = lax.broadcasted_iota(jnp.int32, (512, 512), 1)
    shuffle = (lat == (order % 32) * 16 + order // 32).astype(BF16)
    leg_p[...] = nn(legendre[...], shuffle).astype(BF16)
    shuffle_t = (order == (lat % 32) * 16 + lat // 32).astype(BF16)
    leg_t[...] = nt(shuffle_t, legendre[...]).astype(BF16)
    for j in range(5):
        column = jnp.broadcast_to(damping[:, j * 128 : (j + 1) * 128], (128, 128))
        damp[j * 128 : (j + 1) * 128, :] = column.T

    arrived(field_in, 0, 7)
    heat = field_in[...].reshape(128, 128).astype(F32).T
    sent = (wide[1] * (wide[0] + heat)).astype(BF16)
    send2[...] = sent.reshape(32, 4, 128)
    exchange_band(send2, recv2, 2)

    arrived(recv1, 1, 31)
    trans[...] = recv1[...].reshape(512, 128).astype(F32)
    for l in range(16):
        tall[l * 32 : (l + 1) * 32, :] = trans[pl.ds(l, 32, stride=16), :].astype(BF16)
    damped = (nn(leg_p[...], tall[...]) * damp[...]).astype(BF16)
    trans[...] = nn(leg_t[...], damped)
    for b in range(32):
        back1[b] = trans[pl.ds(b, 16, stride=32), :].astype(BF16)
    exchange_band(back1, home1, 3)

    arrived(recv2, 2, 31)
    wide[0] = recv2[...].reshape(128, 128).astype(F32)
    for row in range(2):
        real = wide[0, pl.ds(row * 2, 32, stride=4), :]
        imag = wide[0, pl.ds(row * 2 + 1, 32, stride=4), :]
        for z in range(8):
            l = z * 2 + row
            rolled = jnp.where(
                lane < 16,
                pltpu.roll(real, (128 - 16 * z) % 128, 1),
                pltpu.roll(imag, (144 - 16 * z) % 128, 1),
            )
            tall[l * 32 : (l + 1) * 32, :] = rolled.astype(BF16)
    damped = (nn(leg_p[...], tall[...]) * damp[...]).astype(BF16)
    out = nn(leg_t[...], damped)
    for row in range(2):
        for part in range(2):
            piece = jnp.zeros((32, 128), F32)
            for z in range(8):
                l = z * 2 + row
                moved = pltpu.roll(out[l * 32 : (l + 1) * 32, :], (16 * z - 16 * part) % 128, 1)
                piece = jnp.where(lane // 16 == z, moved, piece)
            wide[0, pl.ds(row * 2 + part, 32, stride=4), :] = piece
    back2[...] = wide[0].astype(BF16).reshape(32, 4, 128)
    exchange_band(back2, home2, 4)

    arrived(home1, 3, 31)
    trans[...] = home1[...].reshape(512, 128).astype(F32)
    for l in range(16):
        piece = trans[pl.ds(l, 32, stride=16), :].T
        updated[l // 2, l % 2] = piece.astype(BF16).reshape(2, 4, 16, 32)
    arrived(home2, 4, 31)
    wide[0] = home2[...].reshape(128, 128).astype(F32)
    for k in range(4):
        piece = wide[0, pl.ds(k, 32, stride=4), :].T
        updated[:, k // 2, k % 2, 2] = piece.astype(BF16).reshape(8, 16, 32)

    gone(packed, 0, 7)
    gone(send1, 1, 31)
    gone(send2, 2, 31)
    gone(back1, 3, 31)
    gone(back2, 4, 31)


def local(
    column_state, cosine, sunlit, w_in, w_out, w_long, fourier, quadrature, legendre, damping
):
    vmem = pl.BlockSpec(memory_space=pltpu.VMEM)
    smem = pl.BlockSpec(memory_space=pltpu.SMEM)
    table = jnp.asarray(fourier_rows())
    heating, packed = pl.pallas_call(
        radiation,
        out_shape=(
            jax.ShapeDtypeStruct((2560, 128), BF16),
            jax.ShapeDtypeStruct((8, 16, 128), BF16),
        ),
        in_specs=[vmem] * 7,
        out_specs=(vmem, vmem),
        scratch_shapes=[
            pltpu.VMEM((2048, 128), BF16),
            pltpu.VMEM((128, 128), F32),
            pltpu.VMEM((2, 128, 128), F32),
        ],
        compiler_params=pltpu.CompilerParams(vmem_limit_bytes=40 * 2**20),
        name="radiation",
    )(column_state.reshape(2560, 256), cosine, sunlit, w_in, w_out, w_long, table)

    flat = fourier.transpose(0, 2, 3, 4, 1).reshape(2048, 32)
    whole = pltpu.VMEM((32, 16, 128), BF16)
    small = pltpu.VMEM((32, 4, 128), BF16)
    updated = pl.pallas_call(
        spectral_kernel,
        out_shape=jax.ShapeDtypeStruct((8, 2, 2, 4, 16, 32), BF16),
        in_specs=[vmem, vmem, smem, vmem, vmem],
        out_specs=vmem,
        scratch_shapes=[
            pltpu.VMEM((8, 16, 128), BF16),
            whole, whole, whole, whole,
            small, small, small, small,
            pltpu.VMEM((512, 128), F32),
            pltpu.VMEM((512, 128), BF16),
            pltpu.VMEM((2, 128, 128), F32),
            pltpu.VMEM((640, 512), BF16),
            pltpu.VMEM((512, 640), BF16),
            pltpu.VMEM((640, 128), F32),
            pltpu.SemaphoreType.DMA((5,)),
            pltpu.SemaphoreType.DMA((5,)),
        ],
        compiler_params=pltpu.CompilerParams(
            collective_id=0, has_side_effects=True, vmem_limit_bytes=32 * 2**20
        ),
        name="spectral",
    )(packed, flat, quadrature, legendre.reshape(640, 512), damping)
    updated = updated.reshape(16, 2, 4, 16, 32).transpose(0, 4, 1, 2, 3)
    return heating.reshape(2, 1280, 128), updated


def solution(mesh):
    in_specs = (
        P(("band", "field"), None, None),
        P(("band", "field"), None),
        P(("band", "field"), None),
        P(),
        P(),
        P(),
        P("band", None, None, None, "field"),
        P("band"),
        P("band", None, None),
        P("band", None),
    )
    out_specs = (P(("band", "field"), None, None), P("band", None, None, None, "field"))
    return jax.shard_map(local, mesh=mesh, in_specs=in_specs, out_specs=out_specs, check_vma=False)
```

time: 141 us -> 48.4 us (0.34)
  waiting for transfers between devices: 65.9 us -> 0 us
  starting transfers between devices: 43.9 us -> 0 us
  Pallas kernels: 0 us -> 39.7 us
  matrix products: 11.4 us -> 0 us
  local copies, waits for them, and re-layouts: 13.4 us -> 7.6 us
  other arithmetic: 4.61 us -> 0 us
    all_to_all x9 -> x0, waiting for transfers between devices: 65.9 us -> none  [the longest x4 23.8 us: local(): lax.all_to_all(single, 'band', split_axis=1, concat_axis=0, tiled=True)]
    all_to_all x9 -> x0, starting transfers between devices: 43.9 us -> none  [the longest x4 19.4 us: local(): lax.all_to_all(single, 'band', split_axis=1, concat_axis=0, tiled=True)]
    pallas_call x0 -> x2, Pallas kernels: none -> 39.7 us  [the longest x1 27.4 us: local(): pl.pallas_call(spectral_kernel, out_shape=jax.ShapeDtypeStruct((8, 2, 2,...]
    dot_general x6 -> x0, matrix products: 10.7 us -> none  [the longest x1 8.48 us: short_wave(): jnp.einsum('bch,hl->bcl', hidden, w_out, preferred_element_type=jnp.float32)]
    convert_element_type x6 -> x0, other arithmetic: 2.87 us -> none  [the longest x4 2.61 us: local(): jnp.einsum('mnl,mnc->lmc', legendre, damped, preferred_element_type=jnp.f...]
    reshape x2 -> x0, local copies, waits for them, and re-layouts: 2.09 us -> none  [the longest x1 1.9 us: local(): heating = heating.reshape(row_count, lon_count, level_count)]
    unnamed x39 -> x23, local copies, waits for them, and re-layouts: 9.17 us -> 7.6 us
  transfers between devices with their start and end apart: 9 -> 0, of which waited for: 9 -> 0; matrix products, arithmetic and copies ran while one was open for 10% -> 0% of each run, Pallas kernels for 0% -> 0%
where the time goes in v1:
time: 48.4 us; the launch traced here: 48 us
  Pallas kernels  39.7 us (82%)
  local copies, waits for them, and re-layouts  7.6 us (16%)
  between operations  0.67 us (1%)
    pallas_call x1, Pallas kernels, local(): pl.pallas_call(spectral_kernel, out_shape=jax.ShapeDtypeStruct((8, 2, 2,...  27.4 us
    pallas_call x1, Pallas kernels, local(): pl.pallas_call(radiation, out_shape=(jax.ShapeDtypeStruct((2560, 128), BF...  12.3 us
    unnamed x23, local copies, waits for them, and re-layouts  7.6 us

profile of v1, /device:TPU:1, one launch (start us, length us, event | category | flops | bytes accessed | tf_op | source)
XLA Modules:
  0.0 48.0 jit_solution(18060346386812584285)
XLA Ops:
  0.6 0.0 copy-start
  0.6 1.3 %copy-done = bf16[2,1280,256]{2,1,0:T(8,128)(2,1)S(1)} copy-done((bf16[2,1280,256]{2,1,0:T(8,128)(2,1)S(1)}, bf16[2,1280,256]{2,1,0:T(8,128)(2,1)}, u32[]{:S(2)}) %copy-start) | copy-done | bytes 1310744
  2.0 0.0 copy-start.1
  2.0 1.2 %copy-done.1 = bf16[256,2048]{1,0:T(8,128)(2,1)S(1)} copy-done((bf16[256,2048]{1,0:T(8,128)(2,1)S(1)}, bf16[256,2048]{1,0:T(8,128)(2,1)}, u32[]{:S(2)}) %copy-start.1) | copy-done | bytes 1048600
  3.2 0.0 copy-start.3
  3.2 1.0 %copy-done.3 = bf16[2048,128]{1,0:T(8,128)(2,1)S(1)} copy-done((bf16[2048,128]{1,0:T(8,128)(2,1)S(1)}, bf16[2048,128]{1,0:T(8,128)(2,1)}, u32[]{:S(2)}) %copy-start.3) | copy-done | bytes 524312
  4.2 0.0 copy-start.5
  4.2 1.0 %copy-done.5 = bf16[128,1280]{1,0:T(8,128)(2,1)S(1)} copy-done((bf16[128,1280]{1,0:T(8,128)(2,1)S(1)}, bf16[128,1280]{1,0:T(8,128)(2,1)}, u32[]{:S(2)}) %copy-start.5) | copy-done | bytes 327704
  5.2 0.0 copy-start.6
  5.2 0.8 %copy-done.6 = bf16[256,128]{1,0:T(8,128)(2,1)S(1)} copy-done((bf16[256,128]{1,0:T(8,128)(2,1)S(1)}, bf16[256,128]{1,0:T(8,128)(2,1)}, u32[]{:S(2)}) %copy-start.6) | copy-done | bytes 65560
  6.0 0.0 copy-start.7
  6.0 0.7 %copy-done.7 = f32[2,1280]{1,0:T(2,128)S(1)} copy-done((f32[2,1280]{1,0:T(2,128)S(1)}, f32[2,1280]{1,0:T(2,128)}, u32[]{:S(2)}) %copy-start.7) | copy-done | bytes 10264
  6.7 0.0 copy-start.8
  6.7 0.7 %copy-done.8 = s32[2,1280]{1,0:T(2,128)S(1)} copy-done((s32[2,1280]{1,0:T(2,128)S(1)}, s32[2,1280]{1,0:T(2,128)}, u32[]{:S(2)}) %copy-start.8) | copy-done | bytes 10264
  7.4 0.0 copy-start.2
  7.4 0.0 copy-start.4
  7.4 0.0 copy-start.9
  7.4 0.0 copy-start.10
  7.4 12.3 %radiation.1 = (bf16[2560,128]{1,0:T(8,128)(2,1)}, bf16[8,16,128]{2,1,0:T(8,128)(2,1)S(1)}) custom-call(bf16[2560,256]{1,0:T(8,128)(2,1)S(1)} %bitcast.10, f32[2,1280]{1,0:T(2,128)S(1)} %copy-done.7, s32[2,1280]{1,0:T(2,128)S(1)} %copy-done.8, bf16[256,2048]{1,0:T(8,128)(2,1)S(1)} %copy-done.1, bf16[2048,128]{1,0:T(8,128)(2,1)S(1)} %copy-done.3, ...), custom_call_target="tpu_custom_call" | custom-call | tf_op jit(solution)/shard_map/radiation/pallas_call | solution.py:251
  19.8 0.0 copy-done.2
  19.8 0.0 copy-done.4
  19.8 0.0 copy-done.9
  19.8 0.0 copy-done.10
  19.8 27.4 %spectral.1 = bf16[8,2,2,4,16,32]{5,4,3,2,1,0:T(8,128)(2,1)S(1)} custom-call(bf16[8,16,128]{2,1,0:T(8,128)(2,1)S(1)} %get-tuple-element.5.packed, bf16[2048,32]{1,0:T(8,128)(2,1)S(1)} %bitcast.12, f32[16]{0:T(128)S(1)} %copy-done.10, bf16[640,512]{1,0:T(8,128)(2,1)S(1)} %bitcast.11, f32[1,640]{1,0:T(1,128)S(1)} %copy-done.9), custom_call_target="tpu_custom_call" | custom-call | tf_op jit(solution)/shard_map/spectral/pallas_call | solution.py:271
  47.2 0.8 %copy.14 = bf16[16,32,2,4,16]{1,4,3,2,0:T(8,128)(2,1)} copy(bf16[16,32,2,4,16]{1,4,3,2,0:T(8,128)(2,1)S(1)} %bitcast.9) | data formatting | bytes 262144
Async XLA Ops:
  0.6 1.3 %copy-start = (bf16[2,1280,256]{2,1,0:T(8,128)(2,1)S(1)}, bf16[2,1280,256]{2,1,0:T(8,128)(2,1)}, u32[]{:S(2)}) copy-start(bf16[2,1280,256]{2,1,0:T(8,128)(2,1)} %param.11) | copy-start | bytes 3932164
  2.0 1.2 %copy-start.1 = (bf16[256,2048]{1,0:T(8,128)(2,1)S(1)}, bf16[256,2048]{1,0:T(8,128)(2,1)}, u32[]{:S(2)}) copy-start(bf16[256,2048]{1,0:T(8,128)(2,1)} %w_in.1) | copy-start | bytes 3145732
  3.2 1.0 %copy-start.3 = (bf16[2048,128]{1,0:T(8,128)(2,1)S(1)}, bf16[2048,128]{1,0:T(8,128)(2,1)}, u32[]{:S(2)}) copy-start(bf16[2048,128]{1,0:T(8,128)(2,1)} %w_out.1) | copy-start | bytes 1572868
  4.2 1.0 %copy-start.5 = (bf16[128,1280]{1,0:T(8,128)(2,1)S(1)}, bf16[128,1280]{1,0:T(8,128)(2,1)}, u32[]{:S(2)}) copy-start(bf16[128,1280]{1,0:T(8,128)(2,1)} %constant.2.clone.table) | copy-start | bytes 983044
  5.2 0.8 %copy-start.6 = (bf16[256,128]{1,0:T(8,128)(2,1)S(1)}, bf16[256,128]{1,0:T(8,128)(2,1)}, u32[]{:S(2)}) copy-start(bf16[256,128]{1,0:T(8,128)(2,1)} %w_long.1) | copy-start | bytes 196612
  6.0 0.7 %copy-start.7 = (f32[2,1280]{1,0:T(2,128)S(1)}, f32[2,1280]{1,0:T(2,128)}, u32[]{:S(2)}) copy-start(f32[2,1280]{1,0:T(2,128)} %cosine.1) | copy-start | bytes 30724
  6.7 0.7 %copy-start.8 = (s32[2,1280]{1,0:T(2,128)S(1)}, s32[2,1280]{1,0:T(2,128)}, u32[]{:S(2)}) copy-start(s32[2,1280]{1,0:T(2,128)} %sunlit.1) | copy-start | bytes 30724
  7.4 12.4 %copy-start.2 = (bf16[1,640,512]{2,1,0:T(8,128)(2,1)S(1)}, bf16[1,640,512]{2,1,0:T(8,128)(2,1)}, u32[]{:S(2)}) copy-start(bf16[1,640,512]{2,1,0:T(8,128)(2,1)} %param.19) | copy-start | bytes 1966084
  7.4 12.4 %copy-start.4 = (bf16[16,32,2,4,16]{1,4,3,2,0:T(8,128)(2,1)S(1)}, bf16[16,32,2,4,16]{1,4,3,2,0:T(8,128)(2,1)}, u32[]{:S(2)}) copy-start(bf16[16,32,2,4,16]{1,4,3,2,0:T(8,128)(2,1)} %param.17) | copy-start | bytes 393220
  7.4 12.4 %copy-start.9 = (f32[1,640]{1,0:T(1,128)S(1)}, f32[1,640]{1,0:T(1,128)}, u32[]{:S(2)}) copy-start(f32[1,640]{1,0:T(1,128)} %damping.1) | copy-start | bytes 7684
  7.4 12.4 %copy-start.10 = (f32[16]{0:T(128)S(1)}, f32[16]{0:T(128)}, u32[]{:S(2)}) copy-start(f32[16]{0:T(128)} %quad.1) | copy-start | bytes 196

commit v2 on v1

--- a/solution.py
+++ b/solution.py
@@ -13,8 +13,9 @@
 BF16 = jnp.bfloat16
 LON = 1280
 WAVES = 32
-CHUNK = 256
 HCHUNK = 512
+ALL_VMEM = 64 * 2**20 - 65536
+FINISH_VMEM = 2**20
 MESH = pl.DeviceIdType.MESH
 GELU_A = 0.7978845608028654
 GELU_B = 0.7978845608028654 * 0.044715
@@ -34,7 +35,7 @@
     full = np.stack([np.cos(angle), -np.sin(angle)], axis=1) / np.sqrt(LON)
     high = full.astype(ml_dtypes.bfloat16)
     low = (full - high.astype(np.float64)).astype(ml_dtypes.bfloat16)
-    return np.stack([high, low], axis=1).reshape(4 * WAVES, LON)
+    return np.stack([high, low], axis=1).reshape(4 * WAVES, LON).T.copy()
 
 
 def gelu2(x):
@@ -43,55 +44,41 @@
     return x + x * jnp.tanh(inner)
 
 
-def radiation(
-    state, cosine, sunlit, w_in, w_out, w_long, table, heating, packed, half_out, light, acc
+def eye(n):
+    row = lax.broadcasted_iota(jnp.int32, (n, n), 0)
+    return (row == lax.broadcasted_iota(jnp.int32, (n, n), 1)).astype(BF16)
+
+
+def kernel(
+    state_hbm, cosine_hbm, sunlit_hbm, w_in_hbm, w_out_hbm, w_long_hbm, table_hbm,
+    fourier_hbm, quad_hbm, legendre_hbm, damping_hbm,
+    heating, updated,
+    state, cosine, sunlit, w_in, w_out, w_long, table, fourier, quad, legendre, damping,
+    in_t, out_t, long_t, heat_t, packed,
+    field_in, send1, recv1, back1, home1, send2, recv2, back2, home2,
+    trans, tall, wide, leg_p, leg_t, damp, load_sems, send_sems, recv_sems,
 ):
-    half_out[...] = (w_out[...].astype(F32) * 0.5).astype(BF16)
-    lit = sunlit[...].astype(F32) * cosine[...]
-    rows = jnp.concatenate(
-        [lit[:, j * 128 : (j + 1) * 128] for j in range(10)] + [jnp.zeros((108, 128), F32)], axis=0
-    )
-    light[...] = rows.T
-    acc[...] = jnp.zeros_like(acc)
-    lane = lax.broadcasted_iota(jnp.int32, (128, 128), 1)
-
-    def step(index, carry):
-        row = index // 5
-        part = index % 5
-        here = pl.ds(pl.multiple_of(index * CHUNK, CHUNK), CHUNK)
-        x = state[here, :]
-        short = jnp.zeros((CHUNK, 128), F32)
-        for h in range(0, 2048, HCHUNK):
-            hidden = gelu2(nn(x, w_in[:, h : h + HCHUNK]))
-            short = short + nn(hidden, half_out[h : h + HCHUNK, :])
-        long = nn(x, w_long[...])
-        scale = []
-        for g in range(2):
-            wanted = (part * 2 + g) * 2 + row
-            scale.append(jnp.sum(jnp.where(lane == wanted, light[...], 0.0), axis=1, keepdims=True))
-        scale = jnp.concatenate(scale, axis=0)
-        heat = (long + scale * short.astype(BF16).astype(F32)).astype(BF16)
-        heating[here, :] = heat
-        cols = pl.ds(pl.multiple_of(part * CHUNK, CHUNK), CHUNK)
-        acc[row] += nn(table[:, cols], heat)
-        return carry
-
-    lax.fori_loop(0, 10, step, 0)
-    first, second = acc[0], acc[1]
-    wave_row = lax.broadcasted_iota(jnp.int32, (128, 128), 0)
-    both = jnp.where(
-        (wave_row % 4) < 2,
-        first + pltpu.roll(first, 126, 0),
-        second + pltpu.roll(second, 2, 0),
-    )
-    packed[...] = both.T.astype(BF16).reshape(8, 16, 128)
-
-
-def spectral_kernel(
-    packed, fourier, quad, legendre, damping, updated,
-    field_in, send1, recv1, back1, home1, send2, recv2, back2, home2,
-    trans, tall, wide, leg_p, leg_t, damp, send_sems, recv_sems,
-):
+    loads = [
+        pltpu.make_async_copy(source, target, load_sems.at[i])
+        for i, (source, target) in enumerate(
+            (
+                (w_in_hbm, w_in),
+                (w_out_hbm, w_out),
+                (w_long_hbm, w_long),
+                (state_hbm, state),
+                (cosine_hbm, cosine),
+                (sunlit_hbm, sunlit),
+                (table_hbm, table),
+                (fourier_hbm, fourier),
+                (quad_hbm, quad),
+                (legendre_hbm, legendre),
+                (damping_hbm, damping),
+            )
+        )
+    ]
+    for load in loads:
+        load.start()
+
     band = lax.axis_index("band")
     field = lax.axis_index("field")
 
@@ -144,13 +131,45 @@
         part = source.at[pl.ds(0, count)]
         pltpu.make_async_copy(part, part, send_sems.at[slot]).wait()
 
+    loads[0].wait()
+    for h in range(0, 2048, 256):
+        in_t[h : h + 256, :] = nt(eye(256), w_in[:, h : h + 256]).astype(BF16)
+    loads[1].wait()
+    loads[2].wait()
+    out_t[...] = (nt(eye(128), w_out[...]) * 0.5).astype(BF16)
+    long_t[...] = nt(eye(128), w_long[...]).astype(BF16)
+    for load in loads[3:6]:
+        load.wait()
+    x = state[...]
+    short = jnp.zeros((128, 2560), F32)
+    ahead = nt(in_t[:HCHUNK, :], x)
+    for h in range(0, 2048, HCHUNK):
+        raw = ahead
+        if h + HCHUNK < 2048:
+            ahead = nt(in_t[h + HCHUNK : h + 2 * HCHUNK, :], x)
+        short = short + nn(out_t[:, h : h + HCHUNK], gelu2(raw))
+    long = nt(long_t[...], x)
+    light = sunlit[...].astype(F32) * cosine[...]
+    light = jnp.concatenate([light[0:1, :], light[1:2, :]], axis=1)
+    heat_t[...] = (long + light * short.astype(BF16).astype(F32)).astype(BF16)
+
+    loads[6].wait()
+    first = nn(heat_t[:, :LON], table[...])
+    second = nn(heat_t[:, LON:], table[...])
+    wave_lane = lax.broadcasted_iota(jnp.int32, (128, 128), 1)
+    both = jnp.where(
+        (wave_lane % 4) < 2,
+        first + pltpu.roll(first, 126, 1),
+        second + pltpu.roll(second, 2, 1),
+    )
+    packed[...] = both.astype(BF16).reshape(8, 16, 128)
+
     pl.semaphore_wait(barrier, 38)
     exchange_field(packed, field_in, 0)
-
-    eye = (
-        lax.broadcasted_iota(jnp.int32, (32, 32), 0) == lax.broadcasted_iota(jnp.int32, (32, 32), 1)
-    ).astype(BF16)
-    waves = nt(eye, fourier[...])
+    for load in loads[7:]:
+        load.wait()
+
+    waves = nt(eye(32), fourier[...])
     lane = lax.broadcasted_iota(jnp.int32, (32, 128), 1)
     for l in range(16):
         trans[pl.ds(l, 32, stride=16), :] = waves[:, l * 128 : (l + 1) * 128] * quad[l]
@@ -181,6 +200,9 @@
     for j in range(5):
         column = jnp.broadcast_to(damping[:, j * 128 : (j + 1) * 128], (128, 128))
         damp[j * 128 : (j + 1) * 128, :] = column.T
+
+    for j in range(0, 2560, 256):
+        heating[j : j + 256, :] = heat_t[:, j : j + 256].astype(F32).T.astype(BF16)
 
     arrived(field_in, 0, 7)
     heat = field_in[...].reshape(128, 128).astype(F32).T
@@ -242,38 +264,58 @@
     gone(back2, 4, 31)
 
 
+def finish(heating, updated, heating_out, updated_out, sems):
+    copies = []
+    for i in range(4):
+        part = pl.ds(i * 640, 640)
+        copies.append(pltpu.make_async_copy(heating.at[part], heating_out.at[part], sems.at[i]))
+    for i in range(2):
+        part = pl.ds(i * 4, 4)
+        copies.append(pltpu.make_async_copy(updated.at[part], updated_out.at[part], sems.at[4 + i]))
+    for copy in copies:
+        copy.start()
+    for copy in copies:
+        copy.wait()
+
+
 def local(
     column_state, cosine, sunlit, w_in, w_out, w_long, fourier, quadrature, legendre, damping
 ):
+    hbm = pl.BlockSpec(memory_space=pltpu.HBM)
     vmem = pl.BlockSpec(memory_space=pltpu.VMEM)
-    smem = pl.BlockSpec(memory_space=pltpu.SMEM)
-    table = jnp.asarray(fourier_rows())
-    heating, packed = pl.pallas_call(
-        radiation,
-        out_shape=(
-            jax.ShapeDtypeStruct((2560, 128), BF16),
-            jax.ShapeDtypeStruct((8, 16, 128), BF16),
-        ),
-        in_specs=[vmem] * 7,
-        out_specs=(vmem, vmem),
-        scratch_shapes=[
-            pltpu.VMEM((2048, 128), BF16),
-            pltpu.VMEM((128, 128), F32),
-            pltpu.VMEM((2, 128, 128), F32),
-        ],
-        compiler_params=pltpu.CompilerParams(vmem_limit_bytes=40 * 2**20),
-        name="radiation",
-    )(column_state.reshape(2560, 256), cosine, sunlit, w_in, w_out, w_long, table)
-
-    flat = fourier.transpose(0, 2, 3, 4, 1).reshape(2048, 32)
+    anywhere = pl.BlockSpec(memory_space=pl.ANY)
+    operands = (
+        column_state.reshape(2560, 256),
+        cosine,
+        sunlit,
+        w_in,
+        w_out,
+        w_long,
+        jnp.asarray(fourier_rows()),
+        fourier.transpose(0, 2, 3, 4, 1).reshape(2048, 32),
+        quadrature,
+        legendre.reshape(640, 512),
+        damping,
+    )
+    held = [pltpu.VMEM(x.shape, x.dtype) for x in operands]
+    held[8] = pltpu.SMEM((16,), F32)
     whole = pltpu.VMEM((32, 16, 128), BF16)
     small = pltpu.VMEM((32, 4, 128), BF16)
-    updated = pl.pallas_call(
-        spectral_kernel,
-        out_shape=jax.ShapeDtypeStruct((8, 2, 2, 4, 16, 32), BF16),
-        in_specs=[vmem, vmem, smem, vmem, vmem],
-        out_specs=vmem,
-        scratch_shapes=[
+    heating, updated = pl.pallas_call(
+        kernel,
+        out_shape=(
+            pltpu.VMEM((2560, 128), BF16),
+            pltpu.VMEM((8, 2, 2, 4, 16, 32), BF16),
+        ),
+        in_specs=[hbm] * len(operands),
+        out_specs=(vmem, vmem),
+        scratch_shapes=held
+        + [
+            pltpu.VMEM((2048, 256), BF16),
+            pltpu.VMEM((128, 2048), BF16),
+            pltpu.VMEM((128, 256), BF16),
+            pltpu.VMEM((128, 2560), BF16),
+            pltpu.VMEM((8, 16, 128), BF16),
             pltpu.VMEM((8, 16, 128), BF16),
             whole, whole, whole, whole,
             small, small, small, small,
@@ -283,14 +325,27 @@
             pltpu.VMEM((640, 512), BF16),
             pltpu.VMEM((512, 640), BF16),
             pltpu.VMEM((640, 128), F32),
+            pltpu.SemaphoreType.DMA((len(operands),)),
             pltpu.SemaphoreType.DMA((5,)),
             pltpu.SemaphoreType.DMA((5,)),
         ],
         compiler_params=pltpu.CompilerParams(
-            collective_id=0, has_side_effects=True, vmem_limit_bytes=32 * 2**20
+            collective_id=0, has_side_effects=True, vmem_limit_bytes=48 * 2**20
         ),
-        name="spectral",
-    )(packed, flat, quadrature, legendre.reshape(640, 512), damping)
+        name="step",
+    )(*[pltpu.with_memory_space_constraint(x, pltpu.HBM) for x in operands])
+    heating, updated = pl.pallas_call(
+        finish,
+        out_shape=(
+            jax.ShapeDtypeStruct((2560, 128), BF16),
+            jax.ShapeDtypeStruct((8, 2, 2, 4, 16, 32), BF16),
+        ),
+        in_specs=[anywhere] * 2,
+        out_specs=(anywhere, anywhere),
+        scratch_shapes=[pltpu.SemaphoreType.DMA((6,))],
+        compiler_params=pltpu.CompilerParams(vmem_limit_bytes=FINISH_VMEM),
+        name="finish",
+    )(heating, updated)
     updated = updated.reshape(16, 2, 4, 16, 32).transpose(0, 4, 1, 2, 3)
     return heating.reshape(2, 1280, 128), updated
 

time: 48.4 us -> 32.4 us (0.67)
  Pallas kernels: 39.7 us -> 31.7 us
  local copies, waits for them, and re-layouts: 7.6 us -> 0 us
    pallas_call x2, Pallas kernels: 39.7 us -> 31.7 us  [the longest x1 30.6 us: local(): pl.pallas_call(kernel, out_shape=(pltpu.VMEM((2560, 128), BF16), pltpu.VM...]
    unnamed x23 -> x0, local copies, waits for them, and re-layouts: 7.6 us -> none
where the time goes in v2:
time: 32.4 us; the launch traced here: 32.3 us
  Pallas kernels  31.7 us (98%)
  between operations  0.64 us (2%)
    pallas_call x1, Pallas kernels, local(): pl.pallas_call(kernel, out_shape=(pltpu.VMEM((2560, 128), BF16), pltpu.VM...  30.6 us
    pallas_call x1, Pallas kernels, local(): pl.pallas_call(finish, out_shape=(jax.ShapeDtypeStruct((2560, 128), BF16)...  1.06 us

profile of v2, /device:TPU:1, one launch (start us, length us, event | category | flops | bytes accessed | tf_op | source)
XLA Modules:
  0.0 32.3 jit_solution(17476907329792402238)
XLA Ops:
  0.6 30.6 %step.1 = (bf16[2560,128]{1,0:T(8,128)(2,1)S(1)}, bf16[8,2,2,4,16,32]{5,4,3,2,1,0:T(8,128)(2,1)S(1)}) custom-call(bf16[2560,256]{1,0:T(8,128)(2,1)} %bitcast.9, f32[2,1280]{1,0:T(2,128)} %cosine_hbm.1, s32[2,1280]{1,0:T(2,128)} %sunlit_hbm.1, bf16[256,2048]{1,0:T(8,128)(2,1)} %w_in_hbm.1, bf16[2048,128]{1,0:T(8,128)(2,1)} %w_out_hbm.1, ...), custom_call_target="tpu_custom_call" | custom-call | tf_op jit(solution)/shard_map/step/pallas_call | solution.py:304
  31.2 1.1 %finish.1 = (bf16[2560,128]{1,0:T(8,128)(2,1)}, bf16[8,2,2,4,16,32]{5,4,3,2,1,0:T(8,128)(2,1)}) custom-call(bf16[2560,128]{1,0:T(8,128)(2,1)S(1)} %get-tuple-element.6.heating, bf16[8,2,2,4,16,32]{5,4,3,2,1,0:T(8,128)(2,1)S(1)} %get-tuple-element.7.updated), custom_call_target="tpu_custom_call" | custom-call | tf_op jit(solution)/shard_map/finish/pallas_call | solution.py:337

commit v3 on v2

v3 whole, which is shorter than its diff:
```python
import jax
import jax.numpy as jnp
import ml_dtypes
import numpy as np
from jax import lax
from jax.experimental import pallas as pl
from jax.experimental.pallas import tpu as pltpu
from jax.sharding import PartitionSpec as P

F32 = jnp.float32
BF16 = jnp.bfloat16
LON = 1280
WAVES = 32
HCHUNK = 512
CHUNK = 256
ALL_VMEM = 64 * 2**20 - 65536
FINISH_VMEM = 2**20
MESH = pl.DeviceIdType.MESH
GELU_A = 0.7978845608028654
GELU_B = 0.7978845608028654 * 0.044715


def nt(a, b):
    return lax.dot_general(a, b, (((1,), (1,)), ((), ())), preferred_element_type=F32)


def nn(a, b):
    return jnp.dot(a, b, preferred_element_type=F32)


def place(z):
    return (z % 4) * 2 + z // 4


def fourier_rows():
    phase = np.arange(LON)[None, :] * np.arange(WAVES)[:, None] % LON
    angle = 2.0 * np.pi / LON * phase
    full = np.stack([np.cos(angle), -np.sin(angle)]) / np.sqrt(LON)
    high = full.astype(ml_dtypes.bfloat16)
    low = (full - high.astype(np.float64)).astype(ml_dtypes.bfloat16)
    return np.stack([high, low]).reshape(4 * WAVES, 10, 128).swapaxes(0, 1).copy()


def gelu2(x):
    x = x.astype(BF16)
    inner = x * (x * x * BF16(GELU_B) + BF16(GELU_A))
    return x + x * jnp.tanh(inner)


def eye(n):
    row = lax.broadcasted_iota(jnp.int32, (n, n), 0)
    return (row == lax.broadcasted_iota(jnp.int32, (n, n), 1)).astype(BF16)


def kernel(
    state_hbm, cosine_hbm, sunlit_hbm, w_in_hbm, w_out_hbm, w_long_hbm, table_hbm,
    fourier_hbm, quad_hbm, legendre_hbm, damping_hbm,
    heating, updated,
    state, cosine, sunlit, w_in, w_out, w_long, table, fourier, quad, legendre, damping,
    in_t, out_t, hidden, long_wave, heat_t, sent_all, got_all,
    send1, recv1, back1, home1, back2, home2,
    trans, tall, wide, leg_p, leg_t, damp, load_sems, send_sems, recv_sems,
):
    loads = [
        pltpu.make_async_copy(source, target, load_sems.at[i])
        for i, (source, target) in enumerate(
            (
                (w_out_hbm, w_out),
                (w_long_hbm, w_long),
                (w_in_hbm, w_in),
                (state_hbm, state),
                (cosine_hbm, cosine),
                (sunlit_hbm, sunlit),
                (table_hbm, table),
                (quad_hbm, quad),
                (fourier_hbm, fourier),
                (legendre_hbm, legendre),
                (damping_hbm, damping),
            )
        )
    ]
    for load in loads[:6]:
        load.start()

    band = lax.axis_index("band")
    field = lax.axis_index("field")
    x, y, core = band // 8, lax.rem(band // 2, 4), lax.rem(band, 2)

    bands = [
        lax.rem(x + i, 4) * 8 + lax.rem(y + j, 4) * 2 + lax.rem(core + k, 2)
        for i, j in ((2, 2), (2, 1), (2, 3), (1, 2), (3, 2), (2, 0), (0, 2), (1, 1), (1, 3), (3, 1))
        + ((3, 3), (1, 0), (3, 0), (0, 1), (0, 3), (0, 0))
        for k in (1, 0)
    ]

    def ring(start, stop, act):
        def one_field(t, carry):
            near = (t + 1) // 2
            other = lax.rem(field + 12 + near * (1 - 2 * lax.rem(t, 2)), 8)
            for other_band in bands:
                act(other_band, other)
            return carry

        lax.fori_loop(start, stop, one_field, 0)

    def plane(act):
        for other_band in bands[:-1]:
            act(other_band, field)

    barrier = pltpu.get_barrier_semaphore()

    def greet(other_band, other_field):
        pl.semaphore_signal(
            barrier, inc=1, device_id=(other_band, other_field), device_id_type=MESH
        )

    ring(0, 7, greet)
    plane(greet)

    def exchange_band(source, target, slot):
        def one(other_band, other_field):
            pltpu.make_async_remote_copy(
                src_ref=source.at[other_band], dst_ref=target.at[band],
                send_sem=send_sems.at[slot], recv_sem=recv_sems.at[slot],
                device_id=(other_band, other_field), device_id_type=MESH,
            ).start()

        plane(one)
        target[band] = source[band]

    def arrived(target, slot, count):
        part = target.at[pl.ds(0, count)]
        pltpu.make_async_copy(part, part, recv_sems.at[slot]).wait()

    def gone(source, slot, count):
        part = source.at[pl.ds(0, count)]
        pltpu.make_async_copy(part, part, send_sems.at[slot]).wait()

    loads[0].wait()
    loads[1].wait()
    out_t[...] = (nt(eye(128), w_out[...]) * 0.5).astype(BF16)
    in_t[2048:, :] = nt(eye(128), w_long[...]).astype(BF16)
    loads[2].wait()
    for h in range(0, 2048, 256):
        in_t[h : h + 256, :] = nt(eye(256), w_in[:, h : h + 256]).astype(BF16)
    loads[3].wait()
    for load in loads[6:]:
        load.start()
    for h in range(0, 2048, HCHUNK):
        hidden[h : h + HCHUNK, :] = gelu2(nt(in_t[h : h + HCHUNK, :], state[...]))
    long_wave[...] = nt(in_t[2048:, :], state[...])
    loads[4].wait()
    loads[5].wait()
    light = sunlit[...].astype(F32) * cosine[...]
    light = jnp.concatenate([light[0:1, :], light[1:2, :]], axis=1)
    for c in range(0, 2560, CHUNK):
        here = slice(c, c + CHUNK)
        short = nn(out_t[...], hidden[:, here]).astype(BF16).astype(F32)
        heat_t[:, here] = (long_wave[:, here] + light[:, here] * short).astype(BF16)

    loads[6].wait()
    loads[7].wait()
    lane = lax.broadcasted_iota(jnp.int32, (32, 128), 1)
    pieces = []
    rows = jnp.concatenate([table[i] for i in range(10)], axis=1)
    for row in range(2):
        both = nt(rows, heat_t[:, row * LON : (row + 1) * LON])
        weight = quad[field * 2 + row]
        pieces += [(both[i : i + 32, :] + both[i + 64 : i + 96, :]) * weight for i in (0, 32)]
    for z in range(8):
        block = jnp.zeros((32, 128), F32)
        for k in range(4):
            moved = pltpu.roll(pieces[k], (16 * (k - z)) % 128, 1)
            block = jnp.where(lane // 16 == k, moved, block)
        sent_all[z * 32 : (z + 1) * 32, :] = block

    mine = pl.ds(band * 8 + lax.rem(field, 4) * 2 + field // 4, 1)

    def send_heat(other_band, other_field):
        pltpu.make_async_remote_copy(
            src_ref=sent_all.at[pl.ds(other_field * 32 + other_band, 1)], dst_ref=got_all.at[mine],
            send_sem=send_sems.at[0], recv_sem=recv_sems.at[0],
            device_id=(other_band, other_field), device_id_type=MESH,
        ).start()

    pl.semaphore_wait(barrier, 255)
    ring(0, 7, send_heat)
    plane(send_heat)
    got_all[mine, :] = sent_all[pl.ds(field * 32 + band, 1), :]

    loads[8].wait()
    waves = nt(eye(32), fourier[...])
    for l in range(16):
        j = place(l // 2) * 2 + l % 2
        trans[pl.ds(j, 32, stride=16), :] = waves[:, l * 128 : (l + 1) * 128] * quad[l]
    send1[...] = trans[...].astype(BF16).reshape(32, 16, 128)
    exchange_band(send1, recv1, 1)

    loads[9].wait()
    loads[10].wait()

    def latitude(order):
        spot = order % 8
        return order % 256 // 8 * 16 + (spot % 2 * 4 + spot // 2) * 2 + order // 256

    down = lax.broadcasted_iota(jnp.int32, (512, 512), 0)
    across = lax.broadcasted_iota(jnp.int32, (512, 512), 1)
    leg_p[...] = nn(legendre[...], (down == latitude(across)).astype(BF16)).astype(BF16)
    leg_t[...] = nt((across == latitude(down)).astype(BF16), legendre[...]).astype(BF16)
    for j in range(5):
        column = jnp.broadcast_to(damping[:, j * 128 : (j + 1) * 128], (128, 128))
        damp[j * 128 : (j + 1) * 128, :] = column.T
    for j in range(0, 2560, 256):
        heating[j : j + 256, :] = heat_t[:, j : j + 256].astype(F32).T.astype(BF16)

    arrived(recv1, 1, 31)
    trans[...] = recv1[...].reshape(512, 128).astype(F32)
    lane = lax.broadcasted_iota(jnp.int32, (256, 128), 1)
    cool = jnp.zeros((256, 128), F32)
    for row in range(2):
        half = trans[pl.ds(row, 256, stride=2), :]
        tall[row * 256 : (row + 1) * 256, :] = half.astype(BF16)
        for part in range(2):
            k = row * 2 + part
            moved = pltpu.roll(half, (16 * k - 64 * part - 32) % 128, 1)
            cool = jnp.where(lane // 16 == k, moved, cool)
    wide[...] = cool
    damped = (nn(leg_p[...], tall[...]) * damp[...]).astype(BF16)
    out = nn(leg_t[...], damped)
    for row in range(2):
        trans[pl.ds(row, 256, stride=2), :] = out[row * 256 : (row + 1) * 256, :]
    back1[...] = trans[...].astype(BF16).reshape(32, 16, 128)
    exchange_band(back1, home1, 2)

    arrived(got_all, 0, 255)
    warm = wide[...] + got_all[...]
    tall[:256, :] = warm.astype(BF16)
    tall[256:, :] = pltpu.roll(warm, 96, 1).astype(BF16)
    damped = (nn(leg_p[...], tall[...]) * damp[...]).astype(BF16)
    out = nn(leg_t[...], damped)
    wide[...] = jnp.where(lane < 32, out[:256, :], pltpu.roll(out[256:, :], 32, 1))
    pair = jnp.where(
        lane[:128, :] < 64,
        wide[pl.ds(0, 128, stride=2), :],
        pltpu.roll(wide[pl.ds(1, 128, stride=2), :], 64, 1),
    )
    back2[...] = pair.astype(BF16).reshape(32, 4, 128)
    exchange_band(back2, home2, 3)

    arrived(home1, 2, 31)
    trans[...] = home1[...].reshape(512, 128).astype(F32)
    for l in range(16):
        j = place(l // 2) * 2 + l % 2
        piece = trans[pl.ds(j, 32, stride=16), :].T
        updated[l // 2, l % 2] = piece.astype(BF16).reshape(2, 4, 16, 32)
    arrived(home2, 3, 31)
    wide[:128, :] = home2[...].reshape(128, 128).astype(F32)
    for low in range(4):
        piece = wide[pl.ds(low, 32, stride=4), :].T.astype(BF16).reshape(2, 2, 2, 16, 32)
        for high in range(2):
            updated[high * 4 + low, :, :, 2] = piece[high]

    gone(got_all, 0, 255)
    gone(send1, 1, 31)
    gone(back1, 2, 31)
    gone(back2, 3, 31)


def finish(heating, updated, heating_out, updated_out, sems):
    copies = []
    for i in range(4):
        part = pl.ds(i * 640, 640)
        copies.append(pltpu.make_async_copy(heating.at[part], heating_out.at[part], sems.at[i]))
    for i in range(2):
        part = pl.ds(i * 4, 4)
        copies.append(pltpu.make_async_copy(updated.at[part], updated_out.at[part], sems.at[4 + i]))
    for copy in copies:
        copy.start()
    for copy in copies:
        copy.wait()


def local(
    column_state, cosine, sunlit, w_in, w_out, w_long, fourier, quadrature, legendre, damping
):
    hbm = pl.BlockSpec(memory_space=pltpu.HBM)
    vmem = pl.BlockSpec(memory_space=pltpu.VMEM)
    anywhere = pl.BlockSpec(memory_space=pl.ANY)
    operands = (
        column_state.reshape(2560, 256),
        cosine,
        sunlit,
        w_in,
        w_out,
        w_long,
        jnp.asarray(fourier_rows()),
        fourier.transpose(0, 2, 3, 4, 1).reshape(2048, 32),
        quadrature,
        legendre.reshape(640, 512),
        damping,
    )
    held = [pltpu.VMEM(x.shape, x.dtype) for x in operands]
    held[8] = pltpu.SMEM((16,), F32)
    whole = pltpu.VMEM((32, 16, 128), BF16)
    small = pltpu.VMEM((32, 4, 128), BF16)
    heating, updated = pl.pallas_call(
        kernel,
        out_shape=(
            pltpu.VMEM((2560, 128), BF16),
            pltpu.VMEM((8, 2, 2, 4, 16, 32), BF16),
        ),
        in_specs=[hbm] * len(operands),
        out_specs=(vmem, vmem),
        scratch_shapes=held
        + [
            pltpu.VMEM((2176, 256), BF16),
            pltpu.VMEM((128, 2048), BF16),
            pltpu.VMEM((2048, 2560), BF16),
            pltpu.VMEM((128, 2560), F32),
            pltpu.VMEM((128, 2560), BF16),
            pltpu.VMEM((256, 128), F32),
            pltpu.VMEM((256, 128), F32),
            whole, whole, whole, whole,
            small, small,
            pltpu.VMEM((512, 128), F32),
            pltpu.VMEM((512, 128), BF16),
            pltpu.VMEM((256, 128), F32),
            pltpu.VMEM((640, 512), BF16),
            pltpu.VMEM((512, 640), BF16),
            pltpu.VMEM((640, 128), F32),
            pltpu.SemaphoreType.DMA((len(operands),)),
            pltpu.SemaphoreType.DMA((4,)),
            pltpu.SemaphoreType.DMA((4,)),
        ],
        compiler_params=pltpu.CompilerParams(
            collective_id=0, has_side_effects=True, vmem_limit_bytes=48 * 2**20
        ),
        name="step",
    )(*[pltpu.with_memory_space_constraint(x, pltpu.HBM) for x in operands])
    heating, updated = pl.pallas_call(
        finish,
        out_shape=(
            jax.ShapeDtypeStruct((2560, 128), BF16),
            jax.ShapeDtypeStruct((8, 2, 2, 4, 16, 32), BF16),
        ),
        in_specs=[anywhere] * 2,
        out_specs=(anywhere, anywhere),
        scratch_shapes=[pltpu.SemaphoreType.DMA((6,))],
        compiler_params=pltpu.CompilerParams(vmem_limit_bytes=FINISH_VMEM),
        name="finish",
    )(heating, updated)
    updated = updated.reshape(16, 2, 4, 16, 32).transpose(0, 4, 1, 2, 3)
    return heating.reshape(2, 1280, 128), updated


def solution(mesh):
    in_specs = (
        P(("band", "field"), None, None),
        P(("band", "field"), None),
        P(("band", "field"), None),
        P(),
        P(),
        P(),
        P("band", None, None, None, "field"),
        P("band"),
        P("band", None, None),
        P("band", None),
    )
    out_specs = (P(("band", "field"), None, None), P("band", None, None, None, "field"))
    return jax.shard_map(local, mesh=mesh, in_specs=in_specs, out_specs=out_specs, check_vma=False)
```

time: 32.4 us -> 31.7 us (0.978)
  Pallas kernels: 31.7 us -> 31 us
    pallas_call x1, Pallas kernels: 30.6 us -> 29.9 us  [local(): pl.pallas_call(kernel, out_shape=(pltpu.VMEM((2560, 128), BF16), pltpu.VM...]
where the time goes in v3:
time: 31.7 us; the launch traced here: 31.6 us
  Pallas kernels  31 us (98%)
  between operations  0.64 us (2%)
    pallas_call x1, Pallas kernels, local(): pl.pallas_call(kernel, out_shape=(pltpu.VMEM((2560, 128), BF16), pltpu.VM...  29.9 us
    pallas_call x1, Pallas kernels, local(): pl.pallas_call(finish, out_shape=(jax.ShapeDtypeStruct((2560, 128), BF16)...  1.06 us

profile of v3, /device:TPU:1, one launch (start us, length us, event | category | flops | bytes accessed | tf_op | source)
XLA Modules:
  0.0 31.6 jit_solution(16706220019727390188)
XLA Ops:
  0.6 29.9 %step.1 = (bf16[2560,128]{1,0:T(8,128)(2,1)S(1)}, bf16[8,2,2,4,16,32]{5,4,3,2,1,0:T(8,128)(2,1)S(1)}) custom-call(bf16[2560,256]{1,0:T(8,128)(2,1)} %bitcast.9, f32[2,1280]{1,0:T(2,128)} %cosine_hbm.1, s32[2,1280]{1,0:T(2,128)} %sunlit_hbm.1, bf16[256,2048]{1,0:T(8,128)(2,1)} %w_in_hbm.1, bf16[2048,128]{1,0:T(8,128)(2,1)} %w_out_hbm.1, ...), custom_call_target="tpu_custom_call" | custom-call | tf_op jit(solution)/shard_map/step/pallas_call | solution.py:306
  30.6 1.1 %finish.1 = (bf16[2560,128]{1,0:T(8,128)(2,1)}, bf16[8,2,2,4,16,32]{5,4,3,2,1,0:T(8,128)(2,1)}) custom-call(bf16[2560,128]{1,0:T(8,128)(2,1)S(1)} %get-tuple-element.6.heating, bf16[8,2,2,4,16,32]{5,4,3,2,1,0:T(8,128)(2,1)S(1)} %get-tuple-element.7.updated), custom_call_target="tpu_custom_call" | custom-call | tf_op jit(solution)/shard_map/finish/pallas_call | solution.py:340

commit v4 on v3

--- a/solution.py
+++ b/solution.py
@@ -103,6 +103,8 @@
 
         lax.fori_loop(start, stop, one_field, 0)
 
+    fields = [lax.rem(field + i, 8) for i in (4, 3, 5, 2, 6, 1, 7)]
+
     def plane(act):
         for other_band in bands[:-1]:
             act(other_band, field)
@@ -114,7 +116,9 @@
             barrier, inc=1, device_id=(other_band, other_field), device_id_type=MESH
         )
 
-    ring(0, 7, greet)
+    for other_field in fields:
+        for other_band in bands:
+            greet(other_band, other_field)
     plane(greet)
 
     def exchange_band(source, target, slot):

time: 31.7 us -> 31.2 us (0.984)
  Pallas kernels: 31 us -> 30.4 us
    pallas_call x1, Pallas kernels: 29.9 us -> 29.4 us  [local(): pl.pallas_call(kernel, out_shape=(pltpu.VMEM((2560, 128), BF16), pltpu.VM...]
where the time goes in v4:
time: 31.2 us; the launch traced here: 31.1 us
  Pallas kernels  30.4 us (97%)
  between operations  0.64 us (2%)
    pallas_call x1, Pallas kernels, local(): pl.pallas_call(kernel, out_shape=(pltpu.VMEM((2560, 128), BF16), pltpu.VM...  29.4 us
    pallas_call x1, Pallas kernels, local(): pl.pallas_call(finish, out_shape=(jax.ShapeDtypeStruct((2560, 128), BF16)...  1.06 us

profile of v4, /device:TPU:1, one launch (start us, length us, event | category | flops | bytes accessed | tf_op | source)
XLA Modules:
  0.0 31.1 jit_solution(5540269785221430775)
XLA Ops:
  0.6 29.4 %step.1 = (bf16[2560,128]{1,0:T(8,128)(2,1)S(1)}, bf16[8,2,2,4,16,32]{5,4,3,2,1,0:T(8,128)(2,1)S(1)}) custom-call(bf16[2560,256]{1,0:T(8,128)(2,1)} %bitcast.9, f32[2,1280]{1,0:T(2,128)} %cosine_hbm.1, s32[2,1280]{1,0:T(2,128)} %sunlit_hbm.1, bf16[256,2048]{1,0:T(8,128)(2,1)} %w_in_hbm.1, bf16[2048,128]{1,0:T(8,128)(2,1)} %w_out_hbm.1, ...), custom_call_target="tpu_custom_call" | custom-call | tf_op jit(solution)/shard_map/step/pallas_call | solution.py:310
  30.0 1.1 %finish.1 = (bf16[2560,128]{1,0:T(8,128)(2,1)}, bf16[8,2,2,4,16,32]{5,4,3,2,1,0:T(8,128)(2,1)}) custom-call(bf16[2560,128]{1,0:T(8,128)(2,1)S(1)} %get-tuple-element.6.heating, bf16[8,2,2,4,16,32]{5,4,3,2,1,0:T(8,128)(2,1)S(1)} %get-tuple-element.7.updated), custom_call_target="tpu_custom_call" | custom-call | tf_op jit(solution)/shard_map/finish/pallas_call | solution.py:344

commit v5 on v4

--- a/solution.py
+++ b/solution.py
@@ -140,18 +140,16 @@
         part = source.at[pl.ds(0, count)]
         pltpu.make_async_copy(part, part, send_sems.at[slot]).wait()
 
-    loads[0].wait()
-    loads[1].wait()
-    out_t[...] = (nt(eye(128), w_out[...]) * 0.5).astype(BF16)
-    in_t[2048:, :] = nt(eye(128), w_long[...]).astype(BF16)
-    loads[2].wait()
-    for h in range(0, 2048, 256):
-        in_t[h : h + 256, :] = nt(eye(256), w_in[:, h : h + 256]).astype(BF16)
-    loads[3].wait()
+    for load in loads[:4]:
+        load.wait()
     for load in loads[6:]:
         load.start()
     for h in range(0, 2048, HCHUNK):
+        for i in range(h, h + HCHUNK, 256):
+            in_t[i : i + 256, :] = nt(eye(256), w_in[:, i : i + 256]).astype(BF16)
         hidden[h : h + HCHUNK, :] = gelu2(nt(in_t[h : h + HCHUNK, :], state[...]))
+    in_t[2048:, :] = nt(eye(128), w_long[...]).astype(BF16)
+    out_t[...] = (nt(eye(128), w_out[...]) * 0.5).astype(BF16)
     long_wave[...] = nt(in_t[2048:, :], state[...])
     loads[4].wait()
     loads[5].wait()
@@ -272,12 +270,12 @@
 
 def finish(heating, updated, heating_out, updated_out, sems):
     copies = []
-    for i in range(4):
-        part = pl.ds(i * 640, 640)
+    for i in range(1):
+        part = pl.ds(i * 2560, 2560)
         copies.append(pltpu.make_async_copy(heating.at[part], heating_out.at[part], sems.at[i]))
-    for i in range(2):
-        part = pl.ds(i * 4, 4)
-        copies.append(pltpu.make_async_copy(updated.at[part], updated_out.at[part], sems.at[4 + i]))
+    for i in range(1):
+        part = pl.ds(i * 8, 8)
+        copies.append(pltpu.make_async_copy(updated.at[part], updated_out.at[part], sems.at[1 + i]))
     for copy in copies:
         copy.start()
     for copy in copies:
@@ -349,7 +347,7 @@
         ),
         in_specs=[anywhere] * 2,
         out_specs=(anywhere, anywhere),
-        scratch_shapes=[pltpu.SemaphoreType.DMA((6,))],
+        scratch_shapes=[pltpu.SemaphoreType.DMA((2,))],
         compiler_params=pltpu.CompilerParams(vmem_limit_bytes=FINISH_VMEM),
         name="finish",
     )(heating, updated)

time: 31.2 us -> 30.8 us (0.987)
    pallas_call x1, Pallas kernels: 29.4 us -> 29.1 us  [local(): pl.pallas_call(kernel, out_shape=(pltpu.VMEM((2560, 128), BF16), pltpu.VM...]
where the time goes in v5:
time: 30.8 us; the launch traced here: 30.7 us
  Pallas kernels  30.1 us (98%)
  between operations  0.64 us (2%)
    pallas_call x1, Pallas kernels, local(): pl.pallas_call(kernel, out_shape=(pltpu.VMEM((2560, 128), BF16), pltpu.VM...  29.1 us
    pallas_call x1, Pallas kernels, local(): pl.pallas_call(finish, out_shape=(jax.ShapeDtypeStruct((2560, 128), BF16)...  1.03 us

profile of v5, /device:TPU:1, one launch (start us, length us, event | category | flops | bytes accessed | tf_op | source)
XLA Modules:
  0.0 30.7 jit_solution(6282403966864194645)
XLA Ops:
  0.6 29.1 %step.1 = (bf16[2560,128]{1,0:T(8,128)(2,1)S(1)}, bf16[8,2,2,4,16,32]{5,4,3,2,1,0:T(8,128)(2,1)S(1)}) custom-call(bf16[2560,256]{1,0:T(8,128)(2,1)} %bitcast.9, f32[2,1280]{1,0:T(2,128)} %cosine_hbm.1, s32[2,1280]{1,0:T(2,128)} %sunlit_hbm.1, bf16[256,2048]{1,0:T(8,128)(2,1)} %w_in_hbm.1, bf16[2048,128]{1,0:T(8,128)(2,1)} %w_out_hbm.1, ...), custom_call_target="tpu_custom_call" | custom-call | tf_op jit(solution)/shard_map/step/pallas_call | solution.py:308
  29.7 1.0 %finish.1 = (bf16[2560,128]{1,0:T(8,128)(2,1)}, bf16[8,2,2,4,16,32]{5,4,3,2,1,0:T(8,128)(2,1)}) custom-call(bf16[2560,128]{1,0:T(8,128)(2,1)S(1)} %get-tuple-element.6.heating, bf16[8,2,2,4,16,32]{5,4,3,2,1,0:T(8,128)(2,1)S(1)} %get-tuple-element.7.updated), custom_call_target="tpu_custom_call" | custom-call | tf_op jit(solution)/shard_map/finish/pallas_call | solution.py:342
